TPU v7x, 128 devices: a whole 4x4x4 slice. The times are simulated.
128 devices in a mesh: tm: 16 (over x, y), rows: 8 (over z, core).
Axes of the slice: x: 4, y: 4, z: 4, core: 2. Of those that a mesh axis runs over, the one named last changes fastest.
Arguments:
- latents: bfloat16 [32, 64, 64, 384], P('tm', 'rows'), may hold values from -6 to 6
- gain_one: float32 [384], replicated, may hold values from 0.1 to 1.9
- conv_one: bfloat16 [3, 3, 3, 384, 384], replicated, may hold values from -0.0625 to 0.0625
- up_weight: bfloat16 [384, 384], replicated, may hold values from -0.3125 to 0.3125
- gain_two: float32 [192], replicated, may hold values from 0.1 to 1.9
- conv_two: bfloat16 [3, 3, 3, 192, 192], replicated, may hold values from -0.078125 to 0.078125
- frame_counts: int32 [16], replicated, may hold values from 1 to 4, as said below
- row_counts: int32 [8], replicated, may hold values from 4 to 8, as said below
Outputs:
- decoded: bfloat16 [64, 64, 64, 192], P('tm', 'rows')
Inputs may be any that keep to these rules, and one draw needn't show every extreme that they name: The live slots of time shard i are its first frame_counts[i] slots; some shard has 4 live slots and some has one. The frame rows of strip j are its first row_counts[j] row slots; some strip holds 8 rows and some holds 4.
All inputs are finite; a program needn't handle non-finite values.
Results may differ from a plain program's by a relative error of at most 0.0062.
Values may be sent and summed in bfloat16 or wider, within the bound.
A program may use at most 128 MiB of HBM per device.

v0:
```python
import functools

import jax
import jax.numpy as jnp
from jax import lax
from jax.experimental import pallas as pl
from jax.experimental.pallas import tpu as pltpu
from jax.sharding import PartitionSpec as P

MESH = pl.DeviceIdType.MESH
EPS = 1e-06
BF = jnp.bfloat16
F32 = jnp.float32
N_MSG = 20


def rms_silu(wide, gain, scale):
    n = wide.shape[-1]
    mean = jnp.sum(wide * wide, axis=-1, keepdims=True) * (1.0 / n)
    half = wide * (lax.rsqrt(mean + EPS) * (0.5 * scale)) * gain
    return half * (1.0 + jnp.tanh(half))


def column_taps(act):
    width = act.shape[0]
    column = lax.broadcasted_iota(jnp.int32, act.shape, 0)
    left = jnp.where(column == 0, 0.0, pltpu.roll(act, 1, 0))
    right = jnp.where(column == width - 1, 0.0, pltpu.roll(act, width - 1, 0))
    return left, act, right


def kernel(
    n_tm, n_rows,
    frame_counts, row_counts, latents, gain_one, conv_one, up_weight, gain_two, conv_two,
    out,
    x_early, x_late, x_own, xlow, xup, xsend, act_one, w_one, acc_one, w_up_in, w_up,
    ubuf, ybuf, ylow, yup, ysend, m1_send, m2_send, tail_second, tail_last, act_two, w_two, acc_two, obuf,
    send_sem, recv_sem, load_sem, out_sem,
):
    t, r = lax.axis_index("tm"), lax.axis_index("rows")
    later, earlier = (lax.rem(t + 1, n_tm), r), (lax.rem(t + n_tm - 1, n_tm), r)
    lower, upper = (t, lax.rem(r + 1, n_rows)), (t, lax.rem(r + n_rows - 1, n_rows))
    row_count, frame_count = row_counts[r], frame_counts[t]
    last_row = jnp.maximum(row_count - 1, 0)
    strip, width, c1 = x_early.shape
    x_of = (x_early, x_late, x_own.at[0], x_own.at[1])
    tail_of = (tail_second, tail_last)
    c2 = ybuf.shape[-1]
    has_past = (t > 0).astype(F32)
    has_upper = (r > 0).astype(F32)
    has_lower = (r < n_rows - 1).astype(F32)

    def load(k, src, dst):
        return pltpu.make_async_copy(src, dst, load_sem.at[k])

    def message(k, src, dst, to):
        return pltpu.make_async_remote_copy(
            src_ref=src, dst_ref=dst, send_sem=send_sem.at[k], recv_sem=recv_sem.at[k],
            device_id=to, device_id_type=MESH,
        )

    own = load(0, latents, x_own)
    own.start()
    weights_one = {}
    for a in (2, 1, 0):
        for b in range(3):
            k = 1 + 3 * a + b
            weights_one[a, b] = load(
                k, conv_one.at[a, b], w_one.at[b, :, :, pl.ds((2 - a) * c1, c1)]
            )
    load_up = load(10, up_weight, w_up_in)
    weights_two = [
        load(11 + 3 * a + b, conv_two.at[a, b], w_two.at[a, b, pl.ds(0, 3 * c2)]) for a in range(3) for b in range(3)
    ]

    barrier = pltpu.get_barrier_semaphore()
    for place in (later, earlier, lower, upper):
        pl.semaphore_signal(barrier, inc=1, device_id=place, device_id_type=MESH)
    for a in (2, 1, 0):
        for b in range(3):
            weights_one[a, b].start()
    load_up.start()
    for copy in weights_two:
        copy.start()
    pl.semaphore_wait(barrier, 4)

    frame_late = message(0, latents.at[1], x_late, later)
    frame_early = [
        message(1, latents.at[0, 3:8], x_early.at[3:8], later),
        message(2, latents.at[0, 0:1], x_early.at[0:1], later),
        message(3, latents.at[0, 1:3], x_early.at[1:3], later),
    ]
    rim_first = message(4, latents.at[:, 0], xlow.at[2:4], upper)
    rim_last = message(5, xsend.at[2:4], xup.at[2:4], lower)
    rim_first.start()
    frame_late.start()
    for copy in frame_early:
        copy.start()
    own.wait()
    for f in (2, 3):
        xsend[f] = x_of[f][last_row]
    rim_last.start()

    gain_1 = gain_one[...].reshape(1, c1)
    gain_2 = gain_two[...].reshape(1, c2)

    def pack_one(f, first, last, past):
        def step(s, _):
            is_upper, is_lower = s == 0, (s == strip + 1) | (s - 1 == row_count)
            mine = x_of[f][jnp.clip(s - 1, 0, strip - 1)]
            raw = lax.select(is_upper, xup[f], lax.select(is_lower, xlow[f], mine))
            scale = past * jnp.where(is_upper, has_upper, jnp.where(is_lower, has_lower, 1.0))
            taps = column_taps(rms_silu(raw.astype(F32), gain_1, scale))
            for e in range(3):
                act_one[f, s, :, e * c1 : (e + 1) * c1] = taps[e].astype(BF)
            return 0

        lax.fori_loop(first, last, step, 0)

    def pack_inner(f, first, last, past):
        def step(s, _):
            taps = column_taps(rms_silu(x_of[f][s - 1].astype(F32), gain_1, past))
            for e in range(3):
                act_one[f, s, :, e * c1 : (e + 1) * c1] = taps[e].astype(BF)
            return 0

        lax.fori_loop(first, last, step, 0)

    def conv_one_dot(f, row, rows, first, last):
        planes = [act_one[f, row + b : row + b + rows].reshape(rows * width, 3 * c1) for b in range(3)]
        weight = w_one[:, :, :, first * c1 : last * c1].reshape(9 * c1, (last - first) * c1)
        return jnp.dot(jnp.concatenate(planes, axis=1), weight, preferred_element_type=F32)

    for f in (2, 3):
        pack_inner(f, 1, 5, 1.0)
    rim_first.wait_recv()
    rim_last.wait_recv()
    for f in (2, 3):
        pack_one(f, 0, 1, 1.0)
        pack_one(f, 5, 10, 1.0)

    for a in (2, 1):
        for b in range(3):
            weights_one[a, b].wait()
    acc_one[...] = conv_one_dot(2, 0, strip, 0, 2)
    acc_one[:, c1 : 2 * c1] += conv_one_dot(3, 0, strip, 0, 1)
    for b in range(3):
        weights_one[0, b].wait()
    load_up.wait()
    w_up[...] = jnp.zeros_like(w_up)
    w_up[:, 0:c2] = w_up_in[:, 0:c2]
    w_up[:, 256 : 256 + c2] = w_up_in[:, c2 : 2 * c2]

    def forward_rims_one(k, f):
        xsend[f] = x_of[f][last_row]
        first = message(k, x_of[f].at[0], xlow.at[f], upper)
        final = message(k + 1, xsend.at[f], xup.at[f], lower)
        first.start()
        final.start()
        return first, final

    frame_late.wait_recv()
    late_rims = forward_rims_one(6, 1)
    pack_inner(1, 1, 5, has_past)
    for copy in late_rims:
        copy.wait_recv()
    pack_one(1, 0, 1, has_past)
    pack_one(1, 5, 10, has_past)
    acc_one[...] += conv_one_dot(1, 0, strip, 1, 3)

    for copy in weights_two:
        copy.wait()
    w_two[:, :, 3 * c2 :] = jnp.zeros((3, 3, 64, c2), BF)

    def live(slot, row):
        return ((slot < frame_count) & (row < row_count)).astype(F32)

    def middle_rows(row, rows):
        cells = pl.ds(row * width, rows * width)
        acc_one[cells, 0:c1] += conv_one_dot(0, row, rows, 2, 3)
        for f in range(2):
            wide = x_own[f, row : row + rows].reshape(rows * width, c1).astype(F32)
            mid = (wide + acc_one[cells, f * c1 : (f + 1) * c1]).astype(BF)
            pair = jnp.dot(mid, w_up[...], preferred_element_type=F32)
            for s in range(2):
                half = pair[:, 256 * s : 256 * s + c2].astype(BF)
                ubuf[2 * f + s, row : row + rows] = half.reshape(rows, width, c2)

        def step(k, _):
            slot, place = k // rows, row + k % rows
            wide = ubuf[slot, place].astype(F32) * live(slot, place)
            ubuf[slot, place] = wide.astype(BF)
            ybuf[slot, place] = rms_silu(wide, gain_2, 1.0).astype(BF)
            return 0

        lax.fori_loop(0, 4 * rows, step, 0)

    def send_last(k, row, rows):
        def step(place, _):
            m1_send[place] = ybuf[jnp.maximum(frame_count - 1, 0), place]
            return 0

        lax.fori_loop(row, row + rows, step, 0)
        copy = message(k, m1_send.at[row : row + rows], tail_last.at[row : row + rows], later)
        copy.start()
        return copy

    def send_second(k, row, rows):
        def step(place, _):
            second = ybuf[jnp.maximum(frame_count - 2, 0), place]
            passed = (tail_last[place].astype(F32) * has_past).astype(BF)
            m2_send[place] = lax.select(frame_count >= 2, second, passed)
            return 0

        lax.fori_loop(row, row + rows, step, 0)
        copy = message(k, m2_send.at[row : row + rows], tail_second.at[row : row + rows], later)
        copy.start()
        return copy

    half_rows = strip // 2
    for copy in frame_early:
        copy.wait_recv()
    early_rims = forward_rims_one(8, 0)
    pack_inner(0, 1, 5, has_past)
    for copy in early_rims:
        copy.wait_recv()
    pack_one(0, 0, 1, has_past)
    pack_one(0, 5, 10, has_past)
    middle_rows(half_rows, half_rows)
    last_b = send_last(12, half_rows, half_rows)
    middle_rows(0, half_rows)
    last_a = send_last(13, 0, half_rows)

    for f in range(4):
        ysend[2 + f] = ybuf[f, last_row]
    two_first = message(10, ybuf.at[:, 0], ylow.at[2:6], upper)
    two_last = message(11, ysend.at[2:6], yup.at[2:6], lower)
    two_first.start()
    two_last.start()

    def pack_two(f, first, last, past, rows_of):
        def step(s, _):
            is_upper, is_lower = s == 0, (s == strip + 1) | (s - 1 == row_count)
            mine = rows_of(jnp.clip(s - 1, 0, strip - 1))
            raw = lax.select(is_upper, yup[f], lax.select(is_lower, ylow[f], mine))
            scale = past * jnp.where(is_upper, has_upper, jnp.where(is_lower, has_lower, 1.0))
            left, middle, right = column_taps(raw.astype(F32) * scale)
            blank = jnp.zeros((width, 640 - 3 * c2), F32)
            row = jnp.concatenate([left, middle, right, blank], axis=1)
            act_two[f, s] = row.astype(BF)
            return 0

        lax.fori_loop(first, last, step, 0)

    two_first.wait_recv()
    two_last.wait_recv()
    for f in range(4):
        pack_two(2 + f, 0, strip + 2, 1.0, lambda place, f=f: ybuf[f, place])

    last_b.wait_recv()
    second_b = send_second(14, half_rows, half_rows)
    last_a.wait_recv()
    second_a = send_second(15, 0, half_rows)

    def forward_rims_two(k, f):
        ysend[f] = tail_of[f][last_row]
        first = message(k, tail_of[f].at[0], ylow.at[f], upper)
        final = message(k + 1, ysend.at[f], yup.at[f], lower)
        first.start()
        final.start()
        return first, final

    rims_last = forward_rims_two(16, 1)

    def conv_two_dot(frames, taps):
        planes = [
            act_two[f, b : b + strip].reshape(strip * width, 640) for f in frames for b in range(3)
        ]
        weight = w_two[taps[0] : taps[-1] + 1].reshape(len(taps) * 3 * 640, c2)
        return jnp.dot(jnp.concatenate(planes, axis=1), weight, preferred_element_type=F32)

    def finish(q):
        def step(place, _):
            wide = ubuf[q, place].astype(F32)
            conv = acc_two[q % 2, pl.ds(pl.multiple_of(place * width, width), width)]
            obuf[q, place] = ((wide + conv) * live(q, place)).astype(BF)
            return 0

        lax.fori_loop(0, strip, step, 0)
        copy = pltpu.make_async_copy(obuf.at[q], out.at[q], out_sem.at[q])
        copy.start()
        return copy

    written = []
    for q in (3, 2):
        acc_two[q % 2] = conv_two_dot((q, q + 1, q + 2), (0, 1, 2))
        written.append(finish(q))
    acc_two[1] = conv_two_dot((2, 3), (1, 2))
    acc_two[0] = conv_two_dot((2,), (2,))

    for copy in rims_last:
        copy.wait_recv()
    pack_two(1, 0, strip + 2, has_past, lambda place: tail_last[place])
    acc_two[1] += conv_two_dot((1,), (0,))
    written.append(finish(1))
    second_b.wait_recv()
    second_a.wait_recv()
    rims_second = forward_rims_two(18, 0)
    for copy in rims_second:
        copy.wait_recv()
    pack_two(0, 0, strip + 2, has_past, lambda place: tail_second[place])
    acc_two[0] += conv_two_dot((0, 1), (0, 1))
    written.append(finish(0))

    sent = [frame_late, *frame_early, rim_first, rim_last, *late_rims, *early_rims, last_b, last_a]
    sent += [two_first, two_last, second_b, second_a, *rims_last, *rims_second]
    for copy in sent:
        copy.wait_send()
    for copy in written:
        copy.wait()


def on_device(n_tm, n_rows, latents, gain_one, conv_one, up_weight, gain_two, conv_two, frame_counts, row_counts):
    frames, strip, width, c1 = latents.shape
    c2 = gain_two.shape[0]
    slots = 2 * frames
    cells = strip * width
    vmem = pltpu.VMEM
    scratch = [
        vmem((strip, width, c1), BF),
        vmem((strip, width, c1), BF),
        vmem((2, strip, width, c1), BF),
        vmem((4, width, c1), BF),
        vmem((4, width, c1), BF),
        vmem((4, width, c1), BF),
        vmem((4, strip + 2, width, 3 * c1), BF),
        vmem((3, 3, c1, 3 * c1), BF),
        vmem((cells, 2 * c1), F32),
        vmem((c1, 2 * c2), BF),
        vmem((c1, 512), BF),
        vmem((slots, strip, width, c2), BF),
        vmem((slots, strip, width, c2), BF),
        vmem((6, width, c2), BF),
        vmem((6, width, c2), BF),
        vmem((6, width, c2), BF),
        vmem((strip, width, c2), BF),
        vmem((strip, width, c2), BF),
        vmem((strip, width, c2), BF),
        vmem((strip, width, c2), BF),
        vmem((6, strip + 2, width, 640), BF),
        vmem((3, 3, 3 * c2 + 64, c2), BF),
        vmem((2, cells, c2), F32),
        vmem((slots, strip, width, c2), BF),
        pltpu.SemaphoreType.DMA((N_MSG,)),
        pltpu.SemaphoreType.DMA((N_MSG,)),
        pltpu.SemaphoreType.DMA((20,)),
        pltpu.SemaphoreType.DMA((4,)),
    ]
    smem, anywhere = pl.BlockSpec(memory_space=pltpu.SMEM), pl.BlockSpec(memory_space=pl.ANY)
    in_vmem = pl.BlockSpec(memory_space=pltpu.VMEM)
    return pl.pallas_call(
        functools.partial(kernel, n_tm, n_rows),
        out_shape=jax.ShapeDtypeStruct((slots, strip, width, c2), BF),
        in_specs=[smem, smem, anywhere, in_vmem, anywhere, anywhere, in_vmem, anywhere],
        out_specs=anywhere,
        scratch_shapes=scratch,
        compiler_params=pltpu.CompilerParams(
            collective_id=0, has_side_effects=True, vmem_limit_bytes=60 * 2**20
        ),
    )(frame_counts, row_counts, latents, gain_one, conv_one, up_weight, gain_two, conv_two.reshape(3, 3, 3 * c2, c2))


def solution(mesh):
    in_specs = (P("tm", "rows", None, None), P(), P(), P(), P(), P(), P(), P())
    return jax.shard_map(
        functools.partial(on_device, mesh.shape["tm"], mesh.shape["rows"]),
        mesh=mesh, in_specs=in_specs, out_specs=P("tm", "rows", None, None), check_vma=False,
    )
```

profile of v0, /device:TPU:0, one launch (start us, length us, event | category | flops | bytes accessed | tf_op | source)
XLA Modules:
  0.0 68.1 jit_solution(7588588721826139022)
XLA Ops:
  0.0 65.8 %shard_map.82 = bf16[4,8,64,192]{3,2,1,0:T(8,128)(2,1)} custom-call(s32[16]{0:T(128)} %frame_counts.1, s32[8]{0:T(128)} %row_counts.1, bf16[2,8,64,384]{3,2,1,0:T(8,128)(2,1)} %latents.1, f32[384]{0:T(512)} %gain_one.1, bf16[3,3,3,384,384]{4,3,2,1,0:T(8,128)(2,1)} %conv_one.1, bf16[384,384]{1,0:T(8,128)(2,1)} %up_weight.1, f32[192]{0:T(256)} %gain_two.1, ...), custom_call_target="tpu_custom_call" | custom-call | tf_op jit(solution)/shard_map/pallas_call | solution.py:361
  65.8 2.3 %copy.10 = bf16[4,8,64,192]{3,2,1,0:T(8,128)(2,1)} copy(bf16[4,8,64,192]{3,2,1,0:T(8,128)(2,1)} %shard_map.82) | data formatting | bytes 1572864
where the time goes:
time: 68.3 us; the launch traced here: 68.1 us
  Pallas kernels  65.8 us (96%)
  local copies, waits for them, and re-layouts  2.3 us (3%)
    pallas_call x1, Pallas kernels, on_device(): pl.pallas_call(functools.partial(kernel, n_tm, n_rows), out_shape=jax.Sha...  65.8 us
    unnamed x1, local copies, waits for them, and re-layouts  2.3 us

commit v1 on v0

--- a/solution.py
+++ b/solution.py
@@ -11,7 +11,8 @@
 EPS = 1e-06
 BF = jnp.bfloat16
 F32 = jnp.float32
-N_MSG = 20
+N_MSG = 22
+CHUNKS = ((4, 4), (0, 4))
 
 
 def rms_silu(wide, gain, scale):
@@ -33,8 +34,8 @@
     n_tm, n_rows,
     frame_counts, row_counts, latents, gain_one, conv_one, up_weight, gain_two, conv_two,
     out,
-    x_early, x_late, x_own, xlow, xup, xsend, act_one, w_one, acc_one, w_up_in, w_up,
-    ubuf, ybuf, ylow, yup, ysend, m1_send, m2_send, tail_second, tail_last, act_two, w_two, acc_two, obuf,
+    q_send, q_recv, x_late, x_own, xlow, xup, xsend, act_one, w_one, acc_one, w_up_in, w_up,
+    ubuf, ybuf, ylow, yup, low_last, up_last, low_second, up_second, rim_send, ysend, m1_send, m2_send, tail_second, tail_last, act_two, w_two, acc_two, obuf,
     send_sem, recv_sem, load_sem, out_sem,
 ):
     t, r = lax.axis_index("tm"), lax.axis_index("rows")
@@ -42,9 +43,11 @@
     lower, upper = (t, lax.rem(r + 1, n_rows)), (t, lax.rem(r + n_rows - 1, n_rows))
     row_count, frame_count = row_counts[r], frame_counts[t]
     last_row = jnp.maximum(row_count - 1, 0)
-    strip, width, c1 = x_early.shape
-    x_of = (x_early, x_late, x_own.at[0], x_own.at[1])
+    strip, width, c1 = x_late.shape
+    x_of = (None, x_late, x_own.at[0], x_own.at[1])
     tail_of = (tail_second, tail_last)
+    up_of = (up_second, up_last, *(yup.at[f] for f in range(4)))
+    low_of = (low_second, low_last, *(ylow.at[f] for f in range(4)))
     c2 = ybuf.shape[-1]
     has_past = (t > 0).astype(F32)
     has_upper = (r > 0).astype(F32)
@@ -76,7 +79,7 @@
     barrier = pltpu.get_barrier_semaphore()
     for place in (later, earlier, lower, upper):
         pl.semaphore_signal(barrier, inc=1, device_id=place, device_id_type=MESH)
-    for a in (2, 1, 0):
+    for a in (0, 2, 1):
         for b in range(3):
             weights_one[a, b].start()
     load_up.start()
@@ -84,17 +87,15 @@
         copy.start()
     pl.semaphore_wait(barrier, 4)
 
-    frame_late = message(0, latents.at[1], x_late, later)
-    frame_early = [
-        message(1, latents.at[0, 3:8], x_early.at[3:8], later),
-        message(2, latents.at[0, 0:1], x_early.at[0:1], later),
-        message(3, latents.at[0, 1:3], x_early.at[1:3], later),
+    halves = strip // 2
+    received = [
+        message(i, latents.at[1, first:last], x_late.at[first:last], later)
+        for i, (first, last) in enumerate(((0, 1), (halves - 1, strip), (1, halves - 1)))
     ]
-    rim_first = message(4, latents.at[:, 0], xlow.at[2:4], upper)
-    rim_last = message(5, xsend.at[2:4], xup.at[2:4], lower)
+    rim_first = message(6, latents.at[:, 0], xlow.at[2:4], upper)
+    rim_last = message(7, xsend.at[2:4], xup.at[2:4], lower)
     rim_first.start()
-    frame_late.start()
-    for copy in frame_early:
+    for copy in received:
         copy.start()
     own.wait()
     for f in (2, 3):
@@ -115,7 +116,7 @@
                 act_one[f, s, :, e * c1 : (e + 1) * c1] = taps[e].astype(BF)
             return 0
 
-        lax.fori_loop(first, last, step, 0)
+        lax.fori_loop(first, last, step, 0, unroll=True)
 
     def pack_inner(f, first, last, past):
         def step(s, _):
@@ -124,7 +125,7 @@
                 act_one[f, s, :, e * c1 : (e + 1) * c1] = taps[e].astype(BF)
             return 0
 
-        lax.fori_loop(first, last, step, 0)
+        lax.fori_loop(first, last, step, 0, unroll=True)
 
     def conv_one_dot(f, row, rows, first, last):
         planes = [act_one[f, row + b : row + b + rows].reshape(rows * width, 3 * c1) for b in range(3)]
@@ -139,33 +140,40 @@
         pack_one(f, 0, 1, 1.0)
         pack_one(f, 5, 10, 1.0)
 
+    for b in range(3):
+        weights_one[0, b].wait()
+    q_send[...] = conv_one_dot(2, 0, strip, 2, 3).astype(BF).reshape(strip, width, c1)
+    shares = []
+    for i, (row, rows) in enumerate(CHUNKS):
+        shares.append(message(3 + i, q_send.at[row : row + rows], q_recv.at[row : row + rows], later))
+        shares[i].start()
     for a in (2, 1):
         for b in range(3):
             weights_one[a, b].wait()
     acc_one[...] = conv_one_dot(2, 0, strip, 0, 2)
+    def pick_last(rows):
+        row = rows[halves - 1]
+        for place in range(halves, strip):
+            row = lax.select(last_row == place, rows[place], row)
+        return row
+
+    received[0].wait_recv()
+    received[1].wait_recv()
+    xsend[1] = pick_last(x_late)
+    late_rims = [message(8, x_late.at[0], xlow.at[1], upper), message(9, xsend.at[1], xup.at[1], lower)]
+    for copy in late_rims:
+        copy.start()
     acc_one[:, c1 : 2 * c1] += conv_one_dot(3, 0, strip, 0, 1)
-    for b in range(3):
-        weights_one[0, b].wait()
     load_up.wait()
     w_up[...] = jnp.zeros_like(w_up)
     w_up[:, 0:c2] = w_up_in[:, 0:c2]
     w_up[:, 256 : 256 + c2] = w_up_in[:, c2 : 2 * c2]
-
-    def forward_rims_one(k, f):
-        xsend[f] = x_of[f][last_row]
-        first = message(k, x_of[f].at[0], xlow.at[f], upper)
-        final = message(k + 1, xsend.at[f], xup.at[f], lower)
-        first.start()
-        final.start()
-        return first, final
-
-    frame_late.wait_recv()
-    late_rims = forward_rims_one(6, 1)
-    pack_inner(1, 1, 5, has_past)
+    received[2].wait_recv()
+    pack_inner(1, 1, halves + 1, has_past)
     for copy in late_rims:
         copy.wait_recv()
     pack_one(1, 0, 1, has_past)
-    pack_one(1, 5, 10, has_past)
+    pack_one(1, halves + 1, strip + 2, has_past)
     acc_one[...] += conv_one_dot(1, 0, strip, 1, 3)
 
     for copy in weights_two:
@@ -177,10 +185,12 @@
 
     def middle_rows(row, rows):
         cells = pl.ds(row * width, rows * width)
-        acc_one[cells, 0:c1] += conv_one_dot(0, row, rows, 2, 3)
         for f in range(2):
             wide = x_own[f, row : row + rows].reshape(rows * width, c1).astype(F32)
-            mid = (wide + acc_one[cells, f * c1 : (f + 1) * c1]).astype(BF)
+            wide = wide + acc_one[cells, f * c1 : (f + 1) * c1]
+            if f == 0:
+                wide = wide + q_recv[row : row + rows].reshape(rows * width, c1).astype(F32) * has_past
+            mid = wide.astype(BF)
             pair = jnp.dot(mid, w_up[...], preferred_element_type=F32)
             for s in range(2):
                 half = pair[:, 256 * s : 256 * s + c2].astype(BF)
@@ -193,14 +203,14 @@
             ybuf[slot, place] = rms_silu(wide, gain_2, 1.0).astype(BF)
             return 0
 
-        lax.fori_loop(0, 4 * rows, step, 0)
+        lax.fori_loop(0, 4 * rows, step, 0, unroll=4 * rows if rows < 4 else 8)
 
     def send_last(k, row, rows):
         def step(place, _):
             m1_send[place] = ybuf[jnp.maximum(frame_count - 1, 0), place]
             return 0
 
-        lax.fori_loop(row, row + rows, step, 0)
+        lax.fori_loop(row, row + rows, step, 0, unroll=True)
         copy = message(k, m1_send.at[row : row + rows], tail_last.at[row : row + rows], later)
         copy.start()
         return copy
@@ -212,65 +222,49 @@
             m2_send[place] = lax.select(frame_count >= 2, second, passed)
             return 0
 
-        lax.fori_loop(row, row + rows, step, 0)
+        lax.fori_loop(row, row + rows, step, 0, unroll=True)
         copy = message(k, m2_send.at[row : row + rows], tail_second.at[row : row + rows], later)
         copy.start()
         return copy
 
-    half_rows = strip // 2
-    for copy in frame_early:
-        copy.wait_recv()
-    early_rims = forward_rims_one(8, 0)
-    pack_inner(0, 1, 5, has_past)
-    for copy in early_rims:
-        copy.wait_recv()
-    pack_one(0, 0, 1, has_past)
-    pack_one(0, 5, 10, has_past)
-    middle_rows(half_rows, half_rows)
-    last_b = send_last(12, half_rows, half_rows)
-    middle_rows(0, half_rows)
-    last_a = send_last(13, 0, half_rows)
+    last = []
+    for i, (row, rows) in enumerate(CHUNKS):
+        shares[i].wait_recv()
+        middle_rows(row, rows)
+        last.append(send_last(12 + i, row, rows))
 
     for f in range(4):
-        ysend[2 + f] = ybuf[f, last_row]
-    two_first = message(10, ybuf.at[:, 0], ylow.at[2:6], upper)
-    two_last = message(11, ysend.at[2:6], yup.at[2:6], lower)
+        ysend[f] = ybuf[f, last_row]
+    two_first = message(10, ybuf.at[:, 0], ylow, upper)
+    two_last = message(11, ysend.at[0:4], yup, lower)
     two_first.start()
     two_last.start()
+
+    def taps_two(f, s, raw, scale):
+        left, middle, right = column_taps(raw.astype(F32) * scale)
+        blank = jnp.zeros((width, 640 - 3 * c2), F32)
+        act_two[f, s] = jnp.concatenate([left, middle, right, blank], axis=1).astype(BF)
 
     def pack_two(f, first, last, past, rows_of):
         def step(s, _):
             is_upper, is_lower = s == 0, (s == strip + 1) | (s - 1 == row_count)
             mine = rows_of(jnp.clip(s - 1, 0, strip - 1))
-            raw = lax.select(is_upper, yup[f], lax.select(is_lower, ylow[f], mine))
+            raw = lax.select(is_upper, up_of[f][...], lax.select(is_lower, low_of[f][...], mine))
             scale = past * jnp.where(is_upper, has_upper, jnp.where(is_lower, has_lower, 1.0))
-            left, middle, right = column_taps(raw.astype(F32) * scale)
-            blank = jnp.zeros((width, 640 - 3 * c2), F32)
-            row = jnp.concatenate([left, middle, right, blank], axis=1)
-            act_two[f, s] = row.astype(BF)
-            return 0
-
-        lax.fori_loop(first, last, step, 0)
-
-    two_first.wait_recv()
-    two_last.wait_recv()
-    for f in range(4):
-        pack_two(2 + f, 0, strip + 2, 1.0, lambda place, f=f: ybuf[f, place])
-
-    last_b.wait_recv()
-    second_b = send_second(14, half_rows, half_rows)
-    last_a.wait_recv()
-    second_a = send_second(15, 0, half_rows)
-
-    def forward_rims_two(k, f):
-        ysend[f] = tail_of[f][last_row]
-        first = message(k, tail_of[f].at[0], ylow.at[f], upper)
-        final = message(k + 1, ysend.at[f], yup.at[f], lower)
-        first.start()
-        final.start()
-        return first, final
-
-    rims_last = forward_rims_two(16, 1)
+            taps_two(f, s, raw, scale)
+            return 0
+
+        lax.fori_loop(first, last, step, 0, unroll=True)
+
+    def pack_two_inner(f, first, last, past, rows_of):
+        def step(s, _):
+            taps_two(f, s, rows_of(s - 1), past)
+            return 0
+
+        lax.fori_loop(first, last, step, 0, unroll=True)
+
+    def rows_of(f):
+        return lambda place: ybuf[f, place]
 
     def conv_two_dot(frames, taps):
         planes = [
@@ -286,34 +280,59 @@
             obuf[q, place] = ((wide + conv) * live(q, place)).astype(BF)
             return 0
 
-        lax.fori_loop(0, strip, step, 0)
+        lax.fori_loop(0, strip, step, 0, unroll=True)
         copy = pltpu.make_async_copy(obuf.at[q], out.at[q], out_sem.at[q])
         copy.start()
         return copy
 
-    written = []
-    for q in (3, 2):
-        acc_two[q % 2] = conv_two_dot((q, q + 1, q + 2), (0, 1, 2))
-        written.append(finish(q))
-    acc_two[1] = conv_two_dot((2, 3), (1, 2))
-    acc_two[0] = conv_two_dot((2,), (2,))
-
+    def pack_tail(f):
+        of = lambda place: tail_of[f][place]
+        pack_two(f, 0, 1, has_past, of)
+        pack_two_inner(f, 1, halves + 1, has_past, of)
+        pack_two(f, halves + 1, strip + 2, has_past, of)
+
+    written, second = [], []
+    for f in range(4):
+        pack_two_inner(2 + f, 1, halves + 1, 1.0, rows_of(f))
+    for i, (row, rows) in enumerate(CHUNKS[:-1]):
+        last[i].wait_recv()
+        second.append(send_second(15 + i, row, rows))
+    two_first.wait_recv()
+    two_last.wait_recv()
+    for f in range(4):
+        pack_two(2 + f, 0, 1, 1.0, rows_of(f))
+        pack_two(2 + f, halves + 1, strip + 2, 1.0, rows_of(f))
+    acc_two[1] = conv_two_dot((3, 4, 5), (0, 1, 2))
+    last[-1].wait_recv()
+    second.append(send_second(15 + len(CHUNKS) - 1, *CHUNKS[-1]))
+    ysend[4] = pick_last(tail_last)
+    rims_last = [message(18, tail_last.at[0], low_last, upper), message(19, ysend.at[4], up_last, lower)]
+    for copy in rims_last:
+        copy.start()
+    written.append(finish(3))
+    acc_two[0] = conv_two_dot((2, 3, 4), (0, 1, 2))
+    written.append(finish(2))
     for copy in rims_last:
         copy.wait_recv()
-    pack_two(1, 0, strip + 2, has_past, lambda place: tail_last[place])
-    acc_two[1] += conv_two_dot((1,), (0,))
+    own_second = jnp.maximum(frame_count - 2, 0)
+    for i, (of, passed) in enumerate(((yup, up_last), (ylow, low_last))):
+        passed = (passed[...].astype(F32) * has_past).astype(BF)
+        rim_send[i] = lax.select(frame_count >= 2, of[own_second], passed)
+    rims_second = [message(20, rim_send.at[0], up_second, later), message(21, rim_send.at[1], low_second, later)]
+    for copy in rims_second:
+        copy.start()
+    pack_tail(1)
+    acc_two[1] = conv_two_dot((1, 2, 3), (0, 1, 2))
     written.append(finish(1))
-    second_b.wait_recv()
-    second_a.wait_recv()
-    rims_second = forward_rims_two(18, 0)
-    for copy in rims_second:
+    acc_two[0] = conv_two_dot((1, 2), (1, 2))
+    for copy in (*second, *rims_second):
         copy.wait_recv()
-    pack_two(0, 0, strip + 2, has_past, lambda place: tail_second[place])
-    acc_two[0] += conv_two_dot((0, 1), (0, 1))
+    pack_tail(0)
+    acc_two[0] += conv_two_dot((0,), (0,))
     written.append(finish(0))
 
-    sent = [frame_late, *frame_early, rim_first, rim_last, *late_rims, *early_rims, last_b, last_a]
-    sent += [two_first, two_last, second_b, second_a, *rims_last, *rims_second]
+    sent = [*received, rim_first, rim_last, *shares, *late_rims, *last]
+    sent += [two_first, two_last, *second, *rims_last, *rims_second]
     for copy in sent:
         copy.wait_send()
     for copy in written:
@@ -327,6 +346,7 @@
     cells = strip * width
     vmem = pltpu.VMEM
     scratch = [
+        vmem((strip, width, c1), BF),
         vmem((strip, width, c1), BF),
         vmem((strip, width, c1), BF),
         vmem((2, strip, width, c1), BF),
@@ -340,9 +360,14 @@
         vmem((c1, 512), BF),
         vmem((slots, strip, width, c2), BF),
         vmem((slots, strip, width, c2), BF),
-        vmem((6, width, c2), BF),
-        vmem((6, width, c2), BF),
-        vmem((6, width, c2), BF),
+        vmem((4, width, c2), BF),
+        vmem((4, width, c2), BF),
+        vmem((width, c2), BF),
+        vmem((width, c2), BF),
+        vmem((width, c2), BF),
+        vmem((width, c2), BF),
+        vmem((2, width, c2), BF),
+        vmem((5, width, c2), BF),
         vmem((strip, width, c2), BF),
         vmem((strip, width, c2), BF),
         vmem((strip, width, c2), BF),

time: 68.3 us -> 48.4 us (0.71)
  Pallas kernels: 65.8 us -> 45.9 us
    pallas_call x1, Pallas kernels: 65.8 us -> 45.9 us  [on_device(): pl.pallas_call(functools.partial(kernel, n_tm, n_rows), out_shape=jax.Sha...]
where the time goes in v1:
time: 48.4 us; the launch traced here: 48.2 us
  Pallas kernels  45.9 us (95%)
  local copies, waits for them, and re-layouts  2.3 us (5%)
    pallas_call x1, Pallas kernels, on_device(): pl.pallas_call(functools.partial(kernel, n_tm, n_rows), out_shape=jax.Sha...  45.9 us
    unnamed x1, local copies, waits for them, and re-layouts  2.3 us

profile of v1, /device:TPU:0, one launch (start us, length us, event | category | flops | bytes accessed | tf_op | source)
XLA Modules:
  0.0 48.2 jit_solution(9069934738505921759)
XLA Ops:
  0.0 45.9 %shard_map.82 = bf16[4,8,64,192]{3,2,1,0:T(8,128)(2,1)} custom-call(s32[16]{0:T(128)} %frame_counts.1, s32[8]{0:T(128)} %row_counts.1, bf16[2,8,64,384]{3,2,1,0:T(8,128)(2,1)} %latents.1, f32[384]{0:T(512)} %gain_one.1, bf16[3,3,3,384,384]{4,3,2,1,0:T(8,128)(2,1)} %conv_one.1, bf16[384,384]{1,0:T(8,128)(2,1)} %up_weight.1, f32[192]{0:T(256)} %gain_two.1, ...), custom_call_target="tpu_custom_call" | custom-call | tf_op jit(solution)/shard_map/pallas_call | solution.py:386
  45.9 2.3 %copy.10 = bf16[4,8,64,192]{3,2,1,0:T(8,128)(2,1)} copy(bf16[4,8,64,192]{3,2,1,0:T(8,128)(2,1)} %shard_map.82) | data formatting | bytes 1572864

commit v2 on v1

--- a/solution.py
+++ b/solution.py
@@ -35,8 +35,8 @@
     frame_counts, row_counts, latents, gain_one, conv_one, up_weight, gain_two, conv_two,
     out,
     q_send, q_recv, x_late, x_own, xlow, xup, xsend, act_one, w_one, acc_one, w_up_in, w_up,
-    ubuf, ybuf, ylow, yup, low_last, up_last, low_second, up_second, rim_send, ysend, m1_send, m2_send, tail_second, tail_last, act_two, w_two, acc_two, obuf,
-    send_sem, recv_sem, load_sem, out_sem,
+    ubuf, ybuf, ylow, yup, low_last, up_last, low_second, up_second, rim_send, ysend, m1_send, m2_send, tail_second, tail_last, act_two, w_two, acc_two,
+    send_sem, recv_sem, load_sem,
 ):
     t, r = lax.axis_index("tm"), lax.axis_index("rows")
     later, earlier = (lax.rem(t + 1, n_tm), r), (lax.rem(t + n_tm - 1, n_tm), r)
@@ -266,24 +266,41 @@
     def rows_of(f):
         return lambda place: ybuf[f, place]
 
-    def conv_two_dot(frames, taps):
-        planes = [
-            act_two[f, b : b + strip].reshape(strip * width, 640) for f in frames for b in range(3)
-        ]
+    def conv_two_dot(slots, taps, ranges):
+        blocks = []
+        for q in slots:
+            for row, rows in ranges:
+                planes = [
+                    act_two[q + a, row + b : row + b + rows].reshape(rows * width, 640)
+                    for a in taps
+                    for b in range(3)
+                ]
+                blocks.append(jnp.concatenate(planes, axis=1))
         weight = w_two[taps[0] : taps[-1] + 1].reshape(len(taps) * 3 * 640, c2)
-        return jnp.dot(jnp.concatenate(planes, axis=1), weight, preferred_element_type=F32)
+        total = jnp.dot(jnp.concatenate(blocks, axis=0), weight, preferred_element_type=F32)
+        at, shares = 0, []
+        for q in slots:
+            for row, rows in ranges:
+                shares.append((q, slice(row * width, (row + rows) * width), total[at : at + rows * width]))
+                at += rows * width
+        return shares
+
+    def conv_two(slots, taps, ranges=((0, strip),)):
+        for q, cells, share in conv_two_dot(slots, taps, ranges):
+            acc_two[q, cells] = share
+
+    def conv_two_more(slots, taps):
+        for q, cells, share in conv_two_dot(slots, taps, ((0, strip),)):
+            acc_two[q, cells] += share
 
     def finish(q):
         def step(place, _):
             wide = ubuf[q, place].astype(F32)
-            conv = acc_two[q % 2, pl.ds(pl.multiple_of(place * width, width), width)]
-            obuf[q, place] = ((wide + conv) * live(q, place)).astype(BF)
+            conv = acc_two[q, pl.ds(pl.multiple_of(place * width, width), width)]
+            out[q, place] = ((wide + conv) * live(q, place)).astype(BF)
             return 0
 
         lax.fori_loop(0, strip, step, 0, unroll=True)
-        copy = pltpu.make_async_copy(obuf.at[q], out.at[q], out_sem.at[q])
-        copy.start()
-        return copy
 
     def pack_tail(f):
         of = lambda place: tail_of[f][place]
@@ -291,7 +308,7 @@
         pack_two_inner(f, 1, halves + 1, has_past, of)
         pack_two(f, halves + 1, strip + 2, has_past, of)
 
-    written, second = [], []
+    second = []
     for f in range(4):
         pack_two_inner(2 + f, 1, halves + 1, 1.0, rows_of(f))
     for i, (row, rows) in enumerate(CHUNKS[:-1]):
@@ -302,16 +319,16 @@
     for f in range(4):
         pack_two(2 + f, 0, 1, 1.0, rows_of(f))
         pack_two(2 + f, halves + 1, strip + 2, 1.0, rows_of(f))
-    acc_two[1] = conv_two_dot((3, 4, 5), (0, 1, 2))
     last[-1].wait_recv()
     second.append(send_second(15 + len(CHUNKS) - 1, *CHUNKS[-1]))
     ysend[4] = pick_last(tail_last)
     rims_last = [message(18, tail_last.at[0], low_last, upper), message(19, ysend.at[4], up_last, lower)]
     for copy in rims_last:
         copy.start()
-    written.append(finish(3))
-    acc_two[0] = conv_two_dot((2, 3, 4), (0, 1, 2))
-    written.append(finish(2))
+    conv_two((3,), (0, 1, 2))
+    conv_two((2,), (0, 1, 2))
+    finish(3)
+    finish(2)
     for copy in rims_last:
         copy.wait_recv()
     own_second = jnp.maximum(frame_count - 2, 0)
@@ -322,21 +339,19 @@
     for copy in rims_second:
         copy.start()
     pack_tail(1)
-    acc_two[1] = conv_two_dot((1, 2, 3), (0, 1, 2))
-    written.append(finish(1))
-    acc_two[0] = conv_two_dot((1, 2), (1, 2))
+    conv_two((1,), (0, 1, 2))
+    finish(1)
+    conv_two((0,), (1, 2))
     for copy in (*second, *rims_second):
         copy.wait_recv()
     pack_tail(0)
-    acc_two[0] += conv_two_dot((0,), (0,))
-    written.append(finish(0))
+    conv_two_more((0,), (0,))
+    finish(0)
 
     sent = [*received, rim_first, rim_last, *shares, *late_rims, *last]
     sent += [two_first, two_last, *second, *rims_last, *rims_second]
     for copy in sent:
         copy.wait_send()
-    for copy in written:
-        copy.wait()
 
 
 def on_device(n_tm, n_rows, latents, gain_one, conv_one, up_weight, gain_two, conv_two, frame_counts, row_counts):
@@ -374,20 +389,18 @@
         vmem((strip, width, c2), BF),
         vmem((6, strip + 2, width, 640), BF),
         vmem((3, 3, 3 * c2 + 64, c2), BF),
-        vmem((2, cells, c2), F32),
-        vmem((slots, strip, width, c2), BF),
+        vmem((slots, cells, c2), F32),
         pltpu.SemaphoreType.DMA((N_MSG,)),
         pltpu.SemaphoreType.DMA((N_MSG,)),
         pltpu.SemaphoreType.DMA((20,)),
-        pltpu.SemaphoreType.DMA((4,)),
     ]
     smem, anywhere = pl.BlockSpec(memory_space=pltpu.SMEM), pl.BlockSpec(memory_space=pl.ANY)
     in_vmem = pl.BlockSpec(memory_space=pltpu.VMEM)
     return pl.pallas_call(
         functools.partial(kernel, n_tm, n_rows),
-        out_shape=jax.ShapeDtypeStruct((slots, strip, width, c2), BF),
+        out_shape=pltpu.VMEM((slots, strip, width, c2), BF),
         in_specs=[smem, smem, anywhere, in_vmem, anywhere, anywhere, in_vmem, anywhere],
-        out_specs=anywhere,
+        out_specs=in_vmem,
         scratch_shapes=scratch,
         compiler_params=pltpu.CompilerParams(
             collective_id=0, has_side_effects=True, vmem_limit_bytes=60 * 2**20

time: 48.4 us -> 44.7 us (0.924)
  Pallas kernels: 45.9 us -> 43.6 us
  local copies, waits for them, and re-layouts: 2.3 us -> 0.97 us
    pallas_call x1, Pallas kernels: 45.9 us -> 43.6 us  [on_device(): pl.pallas_call(functools.partial(kernel, n_tm, n_rows), out_shape=pltpu.V...]
    unnamed x1, local copies, waits for them, and re-layouts: 2.3 us -> 0.97 us
where the time goes in v2:
time: 44.7 us; the launch traced here: 44.6 us
  Pallas kernels  43.6 us (98%)
  local copies, waits for them, and re-layouts  0.97 us (2%)
    pallas_call x1, Pallas kernels, on_device(): pl.pallas_call(functools.partial(kernel, n_tm, n_rows), out_shape=pltpu.V...  43.6 us
    unnamed x1, local copies, waits for them, and re-layouts  0.97 us

profile of v2, /device:TPU:0, one launch (start us, length us, event | category | flops | bytes accessed | tf_op | source)
XLA Modules:
  0.0 44.6 jit_solution(4851268501111840414)
XLA Ops:
  0.0 43.6 %shard_map.82 = bf16[4,8,64,192]{3,2,1,0:T(8,128)(2,1)S(1)} custom-call(s32[16]{0:T(128)} %frame_counts.1, s32[8]{0:T(128)} %row_counts.1, bf16[2,8,64,384]{3,2,1,0:T(8,128)(2,1)} %latents.1, f32[384]{0:T(512)} %gain_one.1, bf16[3,3,3,384,384]{4,3,2,1,0:T(8,128)(2,1)} %conv_one.1, bf16[384,384]{1,0:T(8,128)(2,1)} %up_weight.1, f32[192]{0:T(256)} %gain_two.1, ...), custom_call_target="tpu_custom_call" | custom-call | tf_op jit(solution)/shard_map/pallas_call | solution.py:399
  43.6 1.0 %copy.10 = bf16[4,8,64,192]{3,2,1,0:T(8,128)(2,1)} copy(bf16[4,8,64,192]{3,2,1,0:T(8,128)(2,1)S(1)} %shard_map.82) | data formatting | bytes 1572864

commit v3 on v2

--- a/solution.py
+++ b/solution.py
@@ -193,17 +193,12 @@
             mid = wide.astype(BF)
             pair = jnp.dot(mid, w_up[...], preferred_element_type=F32)
             for s in range(2):
-                half = pair[:, 256 * s : 256 * s + c2].astype(BF)
-                ubuf[2 * f + s, row : row + rows] = half.reshape(rows, width, c2)
-
-        def step(k, _):
-            slot, place = k // rows, row + k % rows
-            wide = ubuf[slot, place].astype(F32) * live(slot, place)
-            ubuf[slot, place] = wide.astype(BF)
-            ybuf[slot, place] = rms_silu(wide, gain_2, 1.0).astype(BF)
-            return 0
-
-        lax.fori_loop(0, 4 * rows, step, 0, unroll=4 * rows if rows < 4 else 8)
+                for place in range(row, row + rows):
+                    at = (place - row) * width
+                    half = pair[at : at + width, 256 * s : 256 * s + c2].astype(BF)
+                    wide = half.astype(F32) * live(2 * f + s, place)
+                    ubuf[2 * f + s, place] = wide.astype(BF)
+                    ybuf[2 * f + s, place] = rms_silu(wide, gain_2, 1.0).astype(BF)
 
     def send_last(k, row, rows):
         def step(place, _):

time: 44.7 us -> 44.1 us (0.987)
  Pallas kernels: 43.6 us -> 43 us
    pallas_call x1, Pallas kernels: 43.6 us -> 43 us  [on_device(): pl.pallas_call(functools.partial(kernel, n_tm, n_rows), out_shape=pltpu.V...]
where the time goes in v3:
time: 44.1 us; the launch traced here: 44 us
  Pallas kernels  43 us (98%)
  local copies, waits for them, and re-layouts  0.97 us (2%)
    pallas_call x1, Pallas kernels, on_device(): pl.pallas_call(functools.partial(kernel, n_tm, n_rows), out_shape=pltpu.V...  43 us
    unnamed x1, local copies, waits for them, and re-layouts  0.97 us

profile of v3, /device:TPU:0, one launch (start us, length us, event | category | flops | bytes accessed | tf_op | source)
XLA Modules:
  0.0 44.0 jit_solution(4097989362978538584)
XLA Ops:
  0.0 43.0 %shard_map.82 = bf16[4,8,64,192]{3,2,1,0:T(8,128)(2,1)S(1)} custom-call(s32[16]{0:T(128)} %frame_counts.1, s32[8]{0:T(128)} %row_counts.1, bf16[2,8,64,384]{3,2,1,0:T(8,128)(2,1)} %latents.1, f32[384]{0:T(512)} %gain_one.1, bf16[3,3,3,384,384]{4,3,2,1,0:T(8,128)(2,1)} %conv_one.1, bf16[384,384]{1,0:T(8,128)(2,1)} %up_weight.1, f32[192]{0:T(256)} %gain_two.1, ...), custom_call_target="tpu_custom_call" | custom-call | tf_op jit(solution)/shard_map/pallas_call | solution.py:394
  43.1 1.0 %copy.10 = bf16[4,8,64,192]{3,2,1,0:T(8,128)(2,1)} copy(bf16[4,8,64,192]{3,2,1,0:T(8,128)(2,1)S(1)} %shard_map.82) | data formatting | bytes 1572864

commit v4 on v3

--- a/solution.py
+++ b/solution.py
@@ -300,7 +300,6 @@
     def pack_tail(f):
         of = lambda place: tail_of[f][place]
         pack_two(f, 0, 1, has_past, of)
-        pack_two_inner(f, 1, halves + 1, has_past, of)
         pack_two(f, halves + 1, strip + 2, has_past, of)
 
     second = []
@@ -324,6 +323,7 @@
     conv_two((2,), (0, 1, 2))
     finish(3)
     finish(2)
+    pack_two_inner(1, 1, halves + 1, has_past, lambda place: tail_last[place])
     for copy in rims_last:
         copy.wait_recv()
     own_second = jnp.maximum(frame_count - 2, 0)
@@ -337,7 +337,10 @@
     conv_two((1,), (0, 1, 2))
     finish(1)
     conv_two((0,), (1, 2))
-    for copy in (*second, *rims_second):
+    for copy in second:
+        copy.wait_recv()
+    pack_two_inner(0, 1, halves + 1, has_past, lambda place: tail_second[place])
+    for copy in rims_second:
         copy.wait_recv()
     pack_tail(0)
     conv_two_more((0,), (0,))

time: 44.1 us -> 44.2 us (level)
  no operation moved by 1% of the time
where the time goes in v4:
time: 44.2 us; the launch traced here: 44.1 us
  Pallas kernels  43.1 us (98%)
  local copies, waits for them, and re-layouts  0.97 us (2%)
    pallas_call x1, Pallas kernels, on_device(): pl.pallas_call(functools.partial(kernel, n_tm, n_rows), out_shape=pltpu.V...  43.1 us
    unnamed x1, local copies, waits for them, and re-layouts  0.97 us

profile of v4, /device:TPU:0, one launch (start us, length us, event | category | flops | bytes accessed | tf_op | source)
XLA Modules:
  0.0 44.1 jit_solution(18194018574447112376)
XLA Ops:
  0.0 43.1 %shard_map.82 = bf16[4,8,64,192]{3,2,1,0:T(8,128)(2,1)S(1)} custom-call(s32[16]{0:T(128)} %frame_counts.1, s32[8]{0:T(128)} %row_counts.1, bf16[2,8,64,384]{3,2,1,0:T(8,128)(2,1)} %latents.1, f32[384]{0:T(512)} %gain_one.1, bf16[3,3,3,384,384]{4,3,2,1,0:T(8,128)(2,1)} %conv_one.1, bf16[384,384]{1,0:T(8,128)(2,1)} %up_weight.1, f32[192]{0:T(256)} %gain_two.1, ...), custom_call_target="tpu_custom_call" | custom-call | tf_op jit(solution)/shard_map/pallas_call | solution.py:397
  43.1 1.0 %copy.10 = bf16[4,8,64,192]{3,2,1,0:T(8,128)(2,1)} copy(bf16[4,8,64,192]{3,2,1,0:T(8,128)(2,1)S(1)} %shard_map.82) | data formatting | bytes 1572864
